TPU v7x, 32 devices: a whole 2x2x4 slice. The times are simulated.
32 devices in a mesh: groups: 2 (over y), replica: 4 (over x, core), tensor: 4 (over z).
Axes of the slice: x: 2, y: 2, z: 4, core: 2. Of those that a mesh axis runs over, the one named last changes fastest.
Arguments:
- hidden: bfloat16 [2, 64, 16384], P(None, ('groups', 'replica'), 'tensor'), parts along dimension 1, may hold values from -6 to 6
- queries: bfloat16 [2, 64, 16384], P(None, ('groups', 'replica'), 'tensor'), parts along dimension 1, may hold values from -12 to 12
- stored_keys: bfloat16 [64, 256, 1024], P(('groups', 'replica'), 'tensor'), parts along dimension 0, may hold values from -6 to 6
- stored_values: bfloat16 [64, 256, 1024], P(('groups', 'replica'), 'tensor'), parts along dimension 0, may hold values from -6 to 6
- lengths: int32 [64], P(('groups', 'replica')), parts along dimension 0, may hold values from 128 to 256, as said below
- adapter_of_row: int32 [64], P(('groups', 'replica')), parts along dimension 0, may hold values from 0 to 15, as said below
- key_value_weight: bfloat16 [16384, 2048], P('tensor'), may hold values from -0.046875 to 0.046875
- adapter_down_weight: bfloat16 [16, 32, 16384], P('replica', None, 'tensor'), may hold values from -0.046875 to 0.046875
- adapter_up_weight: bfloat16 [16, 16, 2048], P('replica', None, 'tensor'), may hold values from -1.5 to 1.5
Outputs:
- attended: bfloat16 [2, 64, 16384], P(None, ('groups', 'replica'), 'tensor'), parts along dimension 1
- fresh_kv: bfloat16 [2, 64, 2048], P(None, ('groups', 'replica'), 'tensor'), parts along dimension 1
There are 2 independent parts, one for each index of `groups`. A program takes and returns all parts, laid end to end along the dimension named above; an argument that names none is the same for every part. Nothing has to cross between parts.
Inputs may be any that keep to these rules, and one draw needn't show every extreme that they name: Row r's cache is valid at the positions below lengths[r]; some row has exactly 256. `adapter_of_row`: equal within every aligned block of 8 rows.
All inputs are finite; a program needn't handle non-finite values.
Results may differ from a plain program's by a relative error of at most 0.015.
Values may be sent and summed in bfloat16 or wider, within the bound.
A program may use at most 192 MiB of HBM per device.

v0:
```python
import math

import jax
import jax.numpy as jnp
from jax import lax
from jax.sharding import PartitionSpec as P

QUERY_HEADS = 128
KEY_VALUE_HEADS = 8
HEAD_SIZE = 128


MASKED = -1e30


def joined(value, axis, join):
    pieces = jax.tree.map(lambda part: lax.all_gather(part, axis), value)
    head = jax.tree.map(lambda part: part[0], pieces)
    tail = jax.tree.map(lambda part: part[1:], pieces)
    total, _ = lax.scan(lambda total, piece: (join(total, piece), None), head, tail)
    return total


def combine_partial(earlier, later):
    first_top, first_total, first_acc = earlier
    second_top, second_total, second_acc = later
    joined_top = jnp.maximum(first_top, second_top)
    first_factor = jnp.exp(first_top - joined_top)
    second_factor = jnp.exp(second_top - joined_top)
    joined_total = first_total * first_factor + second_total * second_factor
    joined_acc = first_acc * first_factor[..., None] + second_acc * second_factor[..., None]
    return (joined_top, joined_total, joined_acc)


def per_device(
    hidden,
    queries,
    stored_keys,
    stored_values,
    lengths,
    adapter_of_row,
    key_value_weight,
    adapter_down_weight,
    adapter_up_weight,
):
    step_total, row_total, feat_count = hidden.shape
    kv_width = key_value_weight.shape[1]
    key_value_half = kv_width // 2
    column_total = adapter_up_weight.shape[2]
    rank_width = adapter_up_weight.shape[1]
    block_count = row_total // 8
    tensor_index = lax.axis_index("tensor")
    col_start = tensor_index * column_total
    scale = 1.0 / math.sqrt(HEAD_SIZE)
    group_size = QUERY_HEADS // KEY_VALUE_HEADS
    down_all, up_part = (
        lax.all_gather(adapter_down_weight, "replica", axis=0, tiled=True),
        lax.all_gather(adapter_up_weight, "replica", axis=0, tiled=True),
    )
    block_ids = adapter_of_row.reshape(block_count, 8)[:, 0]
    down_used = jnp.take(down_all, block_ids, axis=0)
    grouped = hidden.reshape(step_total, block_count, 8, feat_count)
    low_rank = jnp.einsum("sbrd,bjd->sbrj", grouped, down_used, preferred_element_type=jnp.float32)
    base_part = jnp.dot(
        hidden.reshape(step_total * row_total, feat_count),
        key_value_weight,
        preferred_element_type=jnp.float32,
    )
    base_part = base_part.reshape(step_total, row_total, kv_width)
    up_full = lax.all_gather(up_part, "tensor", axis=2, tiled=True)
    up_used = jnp.take(up_full, block_ids, axis=0).astype(jnp.float32)
    key_delta = jnp.einsum(
        "sbri,bic->sbrc",
        low_rank[..., :rank_width],
        up_used[..., :key_value_half],
        precision=lax.Precision.HIGHEST,
    )
    value_delta = jnp.einsum(
        "sbri,bic->sbrc",
        low_rank[..., rank_width:],
        up_used[..., key_value_half:],
        precision=lax.Precision.HIGHEST,
    )
    low_delta = jnp.concatenate([key_delta, value_delta], axis=-1).reshape(
        step_total, row_total, kv_width
    )
    summed = lax.psum((base_part + low_delta).astype(jnp.bfloat16), "tensor")
    fresh_own = lax.dynamic_slice_in_dim(summed, col_start, column_total, 2)
    query_complete = lax.all_gather(queries, "tensor", axis=2, tiled=True)
    column_span = stored_keys.shape[1]
    positions = tensor_index * column_span + jnp.arange(column_span)
    usable = (positions[None, :] < lengths[:, None])[None, :, None, None, :]
    query_group_rows = query_complete.reshape(
        step_total, row_total, KEY_VALUE_HEADS, group_size, HEAD_SIZE
    )
    key_store_cache = stored_keys.reshape(row_total, column_span, KEY_VALUE_HEADS, HEAD_SIZE)
    value_store_cache = stored_values.reshape(row_total, column_span, KEY_VALUE_HEADS, HEAD_SIZE)
    scores = (
        jnp.einsum(
            "srgqd,rpgd->srgqp",
            query_group_rows,
            key_store_cache,
            preferred_element_type=jnp.float32,
        )
        * scale
    )
    scores = jnp.where(usable, scores, MASKED)
    local_top = jnp.max(scores, axis=-1)
    weights = jnp.where(usable, jnp.exp(scores - local_top[..., None]), 0.0)
    local_total = jnp.sum(weights, axis=-1).reshape(step_total, row_total, QUERY_HEADS)
    local_acc = jnp.einsum(
        "srgqp,rpgd->srgqd",
        weights.astype(jnp.bfloat16),
        value_store_cache,
        preferred_element_type=jnp.float32,
    )
    local_acc = local_acc.reshape(step_total, row_total, QUERY_HEADS, HEAD_SIZE)
    local_top = local_top.reshape(step_total, row_total, QUERY_HEADS)
    heads_here = queries.shape[2] // HEAD_SIZE
    head_start = tensor_index * heads_here
    merged_top, merged_total, merged_acc = joined(
        (local_top, local_total, local_acc), "tensor", combine_partial
    )
    row_top = lax.dynamic_slice_in_dim(merged_top, head_start, heads_here, 2)
    totals = lax.dynamic_slice_in_dim(merged_total, head_start, heads_here, 2)
    weighted = lax.dynamic_slice_in_dim(merged_acc, head_start, heads_here, 2)
    kv_of_head = (head_start + jnp.arange(heads_here)) // group_size
    newest_keys = summed[..., :key_value_half].reshape(
        step_total, row_total, KEY_VALUE_HEADS, HEAD_SIZE
    )
    newest_values = summed[..., key_value_half:].reshape(
        step_total, row_total, KEY_VALUE_HEADS, HEAD_SIZE
    )
    head_keys = jnp.take(newest_keys, kv_of_head, axis=2)
    head_values = jnp.take(newest_values, kv_of_head, axis=2)
    query_own = queries.reshape(step_total, row_total, heads_here, HEAD_SIZE)
    own_scores = (
        jnp.einsum("srhd,jrhd->srhj", query_own, head_keys, preferred_element_type=jnp.float32)
        * scale
    )
    step_index = jnp.arange(step_total)
    causal = (step_index[None, :] <= step_index[:, None])[:, None, None, :]
    own_scores = jnp.where(causal, own_scores, MASKED)
    new_top = jnp.maximum(row_top, jnp.max(own_scores, axis=-1))
    old_factor = jnp.exp(row_top - new_top)
    own_weights = jnp.where(causal, jnp.exp(own_scores - new_top[..., None]), 0.0)
    totals = totals * old_factor + jnp.sum(own_weights, axis=-1)
    own_part = jnp.einsum(
        "srhj,jrhd->srhd",
        own_weights.astype(jnp.bfloat16),
        head_values,
        preferred_element_type=jnp.float32,
    )
    weighted = weighted * old_factor[..., None] + own_part
    attended = (
        (weighted / totals[..., None])
        .astype(jnp.bfloat16)
        .reshape(step_total, row_total, heads_here * HEAD_SIZE)
    )
    return (attended, fresh_own)


def solution(mesh):
    placed = (
        P(None, ("groups", "replica"), "tensor"),
        P(None, ("groups", "replica"), "tensor"),
        P(("groups", "replica"), "tensor", None),
        P(("groups", "replica"), "tensor", None),
        P(("groups", "replica")),
        P(("groups", "replica")),
        P("tensor", None),
        P("replica", None, "tensor"),
        P("replica", None, "tensor"),
    )
    return jax.shard_map(
        per_device,
        mesh=mesh,
        in_specs=placed,
        out_specs=(
            P(None, ("groups", "replica"), "tensor"),
            P(None, ("groups", "replica"), "tensor"),
        ),
        check_vma=False,
    )
```

profile of v0, /device:TPU:0, one launch (start us, length us, event | category | flops | bytes accessed | tf_op | source)
XLA Modules:
  0.0 215.1 jit_solution(7460418062963241158)
XLA Ops:
  7.2 0.0 copy-start
  7.2 0.0 all-gather.6.cloned.1.call-start
  7.2 8.9 %all_gather.25 = bf16[16,16,512]{2,1,0:T(8,128)(2,1)} all-gather(bf16[4,16,512]{2,1,0:T(8,128)(2,1)} %param.21), channel_id=1, replica_groups=mesh['groups'=2,'replica'=4,'tensor'=4] {'replica'}, dimensions={0}, use_global_device_ids=true | all-gather | bytes 327680 | tf_op jit(solution)/shard_map/all_gather | solution.py:58
  16.2 0.0 all-gather.6.cloned.1.call-update
  16.2 0.0 all-gather.8.cloned.1.call-start
  16.3 0.7 all-gather.8.cloned.1.call-update
  17.0 0.0 all-gather.4.cloned.1.call-start
  17.0 21.5 %all_gather.21 = bf16[2,8,16384]{2,1,0:T(8,128)(2,1)S(1)} all-gather(bf16[2,8,4096]{2,1,0:T(8,128)(2,1)} %param.14), channel_id=1, replica_groups=mesh['groups'=2,'replica'=4,'tensor'=4] {'tensor'}, dimensions={2}, use_global_device_ids=true | all-gather | bytes 655360 | tf_op jit(solution)/shard_map/all_gather | solution.py:89
  38.5 0.9 copy.88
  39.4 1.5 copy.87
  40.9 0.3 copy.89
  41.2 0.1 broadcast_compare_fusion
  41.3 0.1 bitcast_bitcast_fusion.1
  41.3 0.1 bitcast_bitcast_fusion
  41.4 1.8 fusion.39
  43.3 0.0 copy-start.6
  43.3 0.5 convolution_bitcast_fusion
  43.7 1.1 copy.66
  44.8 0.0 all-gather.4.cloned.1.call-update
  44.8 0.0 all-reduce.2.cloned.1.call-start
  44.9 0.0 copy-done.6
  45.0 0.8 fusion.19
  45.8 0.1 all_gather_reshape.10
  45.9 13.1 %all_gather.23 = f32[4,2,8,128]{3,2,1,0:T(8,128)S(1)} all-gather(f32[1,2,8,128]{3,2,1,0:T(8,128)S(1)} %all_gather_reshape.10), channel_id=1, replica_groups=mesh['groups'=2,'replica'=4,'tensor'=4] {'tensor'}, dimensions={0}, use_global_device_ids=true | all-gather | bytes 40960 | tf_op jit(solution)/shard_map/all_gather | solution.py:17
  59.0 0.1 all_gather_reshape.9
  59.1 13.1 %all_gather.22 = f32[4,2,8,128]{3,2,1,0:T(8,128)S(1)} all-gather(f32[1,2,8,128]{3,2,1,0:T(8,128)S(1)} %all_gather_reshape.9), channel_id=1, replica_groups=mesh['groups'=2,'replica'=4,'tensor'=4] {'tensor'}, dimensions={0}, use_global_device_ids=true | all-gather | bytes 40960 | tf_op jit(solution)/shard_map/all_gather | solution.py:17
  72.3 0.0 all-gather.6.cloned.1.call-done
  72.3 0.9 dynamic-slice_select_fusion.2
  73.2 11.3 %all-gather.8.cloned.1.call-done = bf16[16,32,4096]{2,1,0:T(8,128)(2,1)} async-done(((bf16[4,32,4096]{2,1,0:T(8,128)(2,1)}), bf16[16,32,4096]{2,1,0:T(8,128)(2,1)}) %all-gather.8.cloned.1.call-update) | async-done | bytes 4194320 | tf_op jit(solution)/shard_map/all_gather | solution.py:57
  84.4 1.1 convolution_bitcast_fusion.4
  85.6 0.2 convolution_bitcast_fusion.2
  85.8 0.2 convolution_bitcast_fusion.3
  86.0 8.7 %fusion.8 = bf16[2,8,2048]{2,1,0:T(8,128)(2,1)} fusion(bf16[2,8,4096]{2,1,0:T(8,128)(2,1)S(1)} %copy-done, bf16[4096,2048]{1,0:T(8,128)(2,1)} %param.19, f32[2,1,8,1024]{3,2,0,1:T(8,128)S(1)} %convolution_bitcast_fusion.2, f32[2,1,8,1024]{3,2,0,1:T(8,128)S(1)} %convolution_bitcast_fusion.3), kind=kOutput, calls=%fused_computation.13 | convolution fusion | flops 268533760 | bytes 17104896 | tf_op jit(solution)/shard_map/dot_general | solution.py:64
  94.7 0.0 all-reduce.2.cloned.1.call-update
  94.7 0.0 slice-start
  94.7 0.0 slice-start.1
  94.7 72.1 %all-gather.4.cloned.1.call-done = f32[4,2,8,128,128]{4,3,2,1,0:T(8,128)} async-done(((f32[1,2,8,128,128]{4,3,2,1,0:T(8,128)}), f32[4,2,8,128,128]{4,3,2,1,0:T(8,128)}) %all-gather.4.cloned.1.call-update) | async-done | bytes 4194320 | tf_op jit(solution)/shard_map/all_gather | solution.py:17
  166.8 1.3 slice_bitcast_fusion
  168.1 3.9 %slice.79 = f32[3,2,8,128,128]{4,3,2,1,0:T(8,128)} slice(f32[4,2,8,128,128]{4,3,2,1,0:T(8,128)} %all-gather.4.cloned.1.call-done), slice={[1:4], [0:2], [0:8], [0:128], [0:128]} | slice | bytes 6291456 | tf_op jit(solution)/shard_map/slice | solution.py:19
  172.1 0.0 slice-done.1
  172.1 6.7 %while.16 = (s32[]{:T(128)}, f32[2,8,128]{2,1,0:T(8,128)S(1)}, f32[2,8,128]{2,1,0:T(8,128)S(1)}, f32[2,8,128,128]{3,2,1,0:T(8,128)S(1)}, f32[3,2,8,128]{3,2,1,0:...) while((s32[]{:T(128)}, f32[2,8,128]{2,1,0:T(8,128)S(1)}, ...), condition=%wide.region_3.4_spmd, body=%wide.region_2.3_spmd.sunk | while | flops 798722 | bytes 3227749 | solution.py:20
  172.1 2.2 %fusion.46 = f32[2,8,128,128]{3,2,1,0:T(8,128)S(1)} fusion(f32[3,2,8,128,128]{4,3,2,1,0:T(8,128)} %get-tuple-element.168, s32[]{:T(128)S(6)} %copy.111, f32[2,8,128,128]{3,2,1,0:T(8,128)S(1)} %get-tuple-element.157, f32[2,8,128]{2,1,0:T(8,128)S(1)} %get-tuple-element.144, f32[2,8,128]{2,1,0:T(8,128)S(1)} %get-tuple-element.145), kind=kLoop, calls=%fused_computation.3.clone.1 | loop fusion | flops 786432 | bytes 3162116 | tf_op jit(solution)/shard_map/while/body/eval_jaxpr/add | solution.py:31
  174.3 2.2 %fusion.46 = f32[2,8,128,128]{3,2,1,0:T(8,128)S(1)} fusion(f32[3,2,8,128,128]{4,3,2,1,0:T(8,128)} %get-tuple-element.168, s32[]{:T(128)S(6)} %copy.111, f32[2,8,128,128]{3,2,1,0:T(8,128)S(1)} %get-tuple-element.157, f32[2,8,128]{2,1,0:T(8,128)S(1)} %get-tuple-element.144, f32[2,8,128]{2,1,0:T(8,128)S(1)} %get-tuple-element.145), kind=kLoop, calls=%fused_computation.3.clone.1 | loop fusion | flops 786432 | bytes 3162116 | tf_op jit(solution)/shard_map/while/body/eval_jaxpr/add | solution.py:31
  176.6 2.2 %fusion.46 = f32[2,8,128,128]{3,2,1,0:T(8,128)S(1)} fusion(f32[3,2,8,128,128]{4,3,2,1,0:T(8,128)} %get-tuple-element.168, s32[]{:T(128)S(6)} %copy.111, f32[2,8,128,128]{3,2,1,0:T(8,128)S(1)} %get-tuple-element.157, f32[2,8,128]{2,1,0:T(8,128)S(1)} %get-tuple-element.144, f32[2,8,128]{2,1,0:T(8,128)S(1)} %get-tuple-element.145), kind=kLoop, calls=%fused_computation.3.clone.1 | loop fusion | flops 786432 | bytes 3162116 | tf_op jit(solution)/shard_map/while/body/eval_jaxpr/add | solution.py:31
  178.8 0.0 copy-start.4
  178.8 0.8 copy.67
  179.6 0.2 copy.68
  179.8 0.2 copy.76
  180.1 22.0 %all-reduce.2.cloned.1.call-done = bf16[2,8,2048]{2,1,0:T(8,128)(2,1)} async-done(((bf16[2,8,2048]{2,1,0:T(8,128)(2,1)}), bf16[2,8,2048]{2,1,0:T(8,128)(2,1)}) %all-reduce.2.cloned.1.call-update) | async-done | bytes 65552 | tf_op jit(solution)/shard_map/psum | solution.py:87
  202.1 0.8 slice_bitcast_fusion.1
  202.9 0.6 gather_fusion.1
  203.5 0.6 gather_fusion
  204.1 0.1 select_bitcast_fusion
  204.2 0.4 fusion.29
  204.7 0.2 copy.71
  204.8 0.1 fusion.32
  204.9 0.1 copy.85
  205.1 0.1 copy.73
  205.2 0.1 fusion.33
  205.3 0.1 copy.86
  205.4 0.2 copy.75
  205.7 0.8 fusion.15
  206.5 0.7 reshape.141
  207.2 1.3 constant_dynamic-slice_fusion
  (26 shorter events, 0.2 us)
Async XLA Ops:
  7.2 77.3 %copy-start = (bf16[2,8,4096]{2,1,0:T(8,128)(2,1)S(1)}, bf16[2,8,4096]{2,1,0:T(8,128)(2,1)}, u32[]{:S(2)}) copy-start(bf16[2,8,4096]{2,1,0:T(8,128)(2,1)} %param.13) | copy-start | bytes 393220
  7.2 33.7 %copy-start.1 = (bf16[8,64,1024]{2,1,0:T(8,128)(2,1)S(1)}, bf16[8,64,1024]{2,1,0:T(8,128)(2,1)}, u32[]{:S(2)}) copy-start(bf16[8,64,1024]{2,1,0:T(8,128)(2,1)} %param.16) | copy-start | bytes 3145732
  7.2 34.0 %copy-start.5 = (s32[8]{0:T(128)S(1)}, s32[8]{0:T(128)}, u32[]{:S(2)}) copy-start(s32[8]{0:T(128)} %param.17) | copy-start | bytes 100
  7.2 65.1 %all-gather.6.cloned.1.call-start = ((), (), s32[]{:S(2)}) async-start(), calls=%async_computation.1 | async-start | bytes 1310720 | tf_op jit(solution)/shard_map/all_gather | solution.py:70
  16.2 68.2 %all-gather.8.cloned.1.call-start = ((), (), s32[]{:S(2)}) async-start(), calls=%async_computation.2 | async-start | bytes 5242880 | tf_op jit(solution)/shard_map/all_gather | solution.py:57
  17.0 149.9 %all-gather.4.cloned.1.call-start = ((), (), s32[]{:S(2)}) async-start(), calls=%async_computation | async-start | bytes 5242880 | tf_op jit(solution)/shard_map/all_gather | solution.py:17
  43.3 1.7 copy-start.6
  44.8 157.3 %all-reduce.2.cloned.1.call-start = ((), (), s32[]{:S(2)}) async-start(), calls=%async_computation.3 | async-start | bytes 131072 | tf_op jit(solution)/shard_map/psum | solution.py:87
  59.0 35.7 %copy-start.2 = (f32[4,2,8,128]{3,2,1,0:T(8,128)}, f32[4,2,8,128]{3,2,1,0:T(8,128)S(1)}, u32[]{:S(2)}) copy-start(f32[4,2,8,128]{3,2,1,0:T(8,128)S(1)} %all_gather.23) | copy-start | bytes 98308
  72.2 22.5 %copy-start.3 = (f32[4,2,8,128]{3,2,1,0:T(8,128)}, f32[4,2,8,128]{3,2,1,0:T(8,128)S(1)}, u32[]{:S(2)}) copy-start(f32[4,2,8,128]{3,2,1,0:T(8,128)S(1)} %all_gather.22) | copy-start | bytes 98308
  94.7 77.4 %slice-start = ((f32[4,2,8,128]{3,2,1,0:T(8,128)}), f32[3,2,8,128]{3,2,1,0:T(8,128)S(1)}, s32[]{:S(2)}) async-start(f32[4,2,8,128]{3,2,1,0:T(8,128)} %copy-done.2), calls=%async_computation.4 | async-start | bytes 49152 | tf_op jit(solution)/shard_map/slice | solution.py:19
  94.7 77.4 %slice-start.1 = ((f32[4,2,8,128]{3,2,1,0:T(8,128)}), f32[3,2,8,128]{3,2,1,0:T(8,128)S(1)}, s32[]{:S(2)}) async-start(f32[4,2,8,128]{3,2,1,0:T(8,128)} %copy-done.3), calls=%async_computation.5 | async-start | bytes 49152 | tf_op jit(solution)/shard_map/slice | solution.py:19
  178.8 25.4 %copy-start.4 = (bf16[2,8,4096]{2,1,0:T(8,128)(2,1)S(1)}, bf16[2,8,4096]{2,1,0:T(8,128)(2,1)}, u32[]{:S(2)}) copy-start(bf16[2,8,4096]{2,1,0:T(8,128)(2,1)} %param.14) | copy-start | bytes 393220
Sparse Core Ops, SparseCore 0:
  16.3 32.9 all-gather.5
  50.8 33.5 all-gather.7
  86.0 80.7 all-gather.3
  169.6 32.5 all-reduce.1
where the time goes:
time: 216 us; the launch traced here: 215 us
  waiting for transfers between devices  106 us (49%)
  blocking collectives  56.7 us (26%)
  local copies, waits for them, and re-layouts  15.4 us (7%)
  between operations  14.2 us (7%)
  matrix products  13.7 us (6%)
  other arithmetic  8.73 us (4%)
    all_gather x1, waiting for transfers between devices, joined(): pieces = jax.tree.map(lambda part: lax.all_gather(part, axis), value)  72.1 us
    all_gather x2, blocking collectives, joined(): pieces = jax.tree.map(lambda part: lax.all_gather(part, axis), value)  26.2 us
    psum x1, waiting for transfers between devices, per_device(): summed = lax.psum((base_part + low_delta).astype(jnp.bfloat16), 'tensor')  22 us
    all_gather x1, blocking collectives, per_device(): query_complete = lax.all_gather(queries, 'tensor', axis=2, tiled=True)  21.5 us
    all_gather x1, waiting for transfers between devices, per_device(): lax.all_gather(adapter_down_weight, 'replica', axis=0, tiled=True)  11.3 us
    all_gather x1, blocking collectives, per_device(): lax.all_gather(adapter_up_weight, 'replica', axis=0, tiled=True)  8.94 us
    dot_general x1, matrix products, per_device(): jnp.dot(hidden.reshape(step_total * row_total, feat_count), key_value_wei...  8.68 us
    add x3, other arithmetic, combine_partial(): first_acc * first_factor[..., None] + second_acc * second_factor[..., None]  6.6 us
  transfers between devices with their start and end apart: 4, of which 3 were waited for; matrix products, arithmetic and copies ran while one was open for 15% of the time, Pallas kernels for 0%

commit v1 on v0

--- a/solution.py
+++ b/solution.py
@@ -1,8 +1,11 @@
+import functools
 import math
 
 import jax
 import jax.numpy as jnp
 from jax import lax
+from jax.experimental import pallas as pl
+from jax.experimental.pallas import tpu as pltpu
 from jax.sharding import PartitionSpec as P
 
 QUERY_HEADS = 128
@@ -160,6 +163,412 @@
     return (attended, fresh_own)
 
 
+MESH = pl.DeviceIdType.MESH
+GROUP = QUERY_HEADS // KEY_VALUE_HEADS
+CHUNKS = 8
+
+
+def fused_kernel(
+    tensor_size,
+    replica_size,
+    row_total,
+    lengths_ref,
+    ids_ref,
+    hidden_ref,
+    query_ref,
+    up_ref,
+    key_hbm,
+    value_hbm,
+    down_hbm,
+    weight_hbm,
+    out_ref,
+    fresh_ref,
+    key_buf,
+    value_buf,
+    down_buf,
+    weight_buf,
+    query_in,
+    hidden_in,
+    ids_in,
+    base_out,
+    base_in,
+    low_out,
+    low_in,
+    up_wide,
+    delta_out,
+    delta_in,
+    fresh_all,
+    acc_out,
+    acc_in,
+    lse_out,
+    lse_in,
+    local_sem,
+    weight_sem,
+    t_send,
+    t_recv,
+    r_send,
+    r_recv,
+):
+    T, R = tensor_size, replica_size
+    t = lax.axis_index("tensor")
+    r = lax.axis_index("replica")
+    tokens, feat = hidden_ref.shape
+    steps = tokens // row_total
+    columns = up_ref.shape[2]
+    ranks = up_ref.shape[1]
+    adapters = up_ref.shape[0]
+    span = key_buf.shape[1]
+    blocks = query_ref.shape[0] // (row_total * steps * GROUP)
+    per_row = steps * GROUP
+    per_block = row_total * per_row
+    scale = 1.0 / math.sqrt(HEAD_SIZE)
+    depth = feat // CHUNKS
+
+    local = [
+        pltpu.make_async_copy(down_hbm, down_buf, local_sem.at[0]),
+        pltpu.make_async_copy(key_hbm, key_buf, local_sem.at[1]),
+        pltpu.make_async_copy(value_hbm, value_buf, local_sem.at[2]),
+    ]
+    weights = [
+        pltpu.make_async_copy(
+            weight_hbm.at[pl.ds(c * depth, depth)],
+            weight_buf.at[pl.ds(c * depth, depth)],
+            weight_sem.at[c],
+        )
+        for c in range(CHUNKS)
+    ]
+    for copy in weights[:2] + local + weights[2:]:
+        copy.start()
+
+    def along_t(kind, k, src, dst, sign=1):
+        return pltpu.make_async_remote_copy(
+            src_ref=src,
+            dst_ref=dst,
+            send_sem=t_send.at[kind, k],
+            recv_sem=t_recv.at[kind, k],
+            device_id={"tensor": lax.rem(t + sign * k + T, T)},
+            device_id_type=MESH,
+        )
+
+    def along_r(kind, k, src, dst):
+        return pltpu.make_async_remote_copy(
+            src_ref=src,
+            dst_ref=dst,
+            send_sem=r_send.at[kind, k],
+            recv_sem=r_recv.at[kind, k],
+            device_id={"replica": lax.rem(r + k, R)},
+            device_id_type=MESH,
+        )
+
+    lane = lax.broadcasted_iota(jnp.int32, (row_total, 128), 1)
+    sub = lax.broadcasted_iota(jnp.int32, (row_total, 128), 0)
+    ids = jnp.zeros((row_total, 128), jnp.int32)
+    for i in range(row_total):
+        ids = jnp.where(sub == i, ids_ref[i], ids)
+    ids_in[0] = ids
+
+    barrier = pltpu.get_barrier_semaphore()
+    for k in range(1, T):
+        pl.semaphore_signal(
+            barrier, inc=1, device_id={"tensor": lax.rem(t + k, T)}, device_id_type=MESH
+        )
+    for k in range(1, R):
+        pl.semaphore_signal(
+            barrier, inc=1, device_id={"replica": lax.rem(r + k, R)}, device_id_type=MESH
+        )
+    pl.semaphore_wait(barrier, T - 1 + R - 1)
+
+    started = []
+
+    def start(copy):
+        copy.start()
+        started.append(copy)
+        return copy
+
+    hidden_moves = [start(along_r(0, k, hidden_ref, hidden_in.at[k - 1])) for k in range(1, R)]
+    query_moves = [start(along_t(0, k, query_ref, query_in.at[k - 1])) for k in range(1, T)]
+    ids_moves = [start(along_r(1, k, ids_in.at[0], ids_in.at[k])) for k in range(1, R)]
+
+    up_wide[...] = jnp.zeros_like(up_wide)
+    half = (t * columns) // (T * columns // 2)
+    for a in range(adapters):
+        up_wide[a, pl.ds(pl.multiple_of(half * ranks, ranks), ranks), :] = up_ref[a]
+
+    total = None
+    for c in range(CHUNKS):
+        weights[c].wait()
+        part = jnp.dot(
+            hidden_ref[:, c * depth : (c + 1) * depth],
+            weight_buf[c * depth : (c + 1) * depth, :],
+            preferred_element_type=jnp.float32,
+        )
+        total = part if total is None else total + part
+    for u in range(T):
+        base_out[u] = total[:, u * columns : (u + 1) * columns].astype(base_out.dtype)
+    base_moves = [
+        start(along_t(1, k, base_out.at[lax.rem(t + k, T)], base_in.at[k - 1]))
+        for k in range(1, T)
+    ]
+
+    local[0].wait()
+    contract = (((1,), (1,)), ((), ()))
+    for k in range(R):
+        if k > 0:
+            hidden_moves[k - 1].wait_recv()
+        tokens_here = hidden_ref[...] if k == 0 else hidden_in[k - 1]
+        low_out[k] = lax.dot_general(
+            tokens_here, down_buf[...], contract, preferred_element_type=jnp.float32
+        )
+    low_moves = [start(along_t(2, k, low_out, low_in.at[k - 1])) for k in range(1, T)]
+
+    local[1].wait()
+    local[2].wait()
+    place = t * span + lax.broadcasted_iota(jnp.int32, (per_row, span), 1)
+    lse_lane = lax.broadcasted_iota(jnp.int32, (per_row, 128), 1)
+
+    def attend(owner, query, slot):
+        lse = jnp.full((per_row, 128), MASKED, jnp.float32)
+        for b in range(blocks):
+            cols = pl.ds(pl.multiple_of((owner * blocks + b) * HEAD_SIZE, HEAD_SIZE), HEAD_SIZE)
+            for i in range(row_total):
+                first = b * per_block + i * per_row
+                usable = place < lengths_ref[i]
+                scores = scale * lax.dot_general(
+                    query[first : first + per_row, :],
+                    key_buf[i, :, cols],
+                    contract,
+                    preferred_element_type=jnp.float32,
+                )
+                scores = jnp.where(usable, scores, MASKED)
+                top = jnp.max(scores, axis=1, keepdims=True)
+                wide = jnp.where(usable, jnp.exp(scores - top), 0.0)
+                whole = jnp.maximum(jnp.sum(wide, axis=1, keepdims=True), 1.0)
+                acc = jnp.dot(
+                    wide.astype(jnp.bfloat16),
+                    value_buf[i, :, cols],
+                    preferred_element_type=jnp.float32,
+                )
+                acc_out[slot, first : first + per_row, :] = (acc / whole).astype(jnp.bfloat16)
+                lse = jnp.where(lse_lane == b * row_total + i, top + jnp.log(whole), lse)
+        lse_out[slot] = lse
+
+    acc_moves, lse_moves = [], []
+    for k in range(1, T):
+        query_moves[k - 1].wait_recv()
+        attend(lax.rem(t - k + T, T), query_in.at[k - 1], k)
+        acc_moves.append(start(along_t(3, k, acc_out.at[k], acc_in.at[k - 1], -1)))
+        lse_moves.append(start(along_t(4, k, lse_out.at[k], lse_in.at[k - 1], -1)))
+
+    for move in low_moves:
+        move.wait_recv()
+    for move in ids_moves:
+        move.wait_recv()
+    wide_up = up_wide[...].reshape(adapters * 2 * ranks, columns)
+    for k in range(R):
+        low = low_out[k]
+        for j in range(T - 1):
+            low = low + low_in[j, k]
+        mine = ids_in[k] == r * adapters + lane // (2 * ranks)
+        low = jnp.where(jnp.concatenate([mine] * steps, axis=0), low, 0.0)
+        high = low.astype(jnp.bfloat16)
+        rest = (low - high.astype(jnp.float32)).astype(jnp.bfloat16)
+        delta_out[k] = jnp.dot(high, wide_up, preferred_element_type=jnp.float32) + jnp.dot(
+            rest, wide_up, preferred_element_type=jnp.float32
+        )
+    delta_moves = []
+    for k in range(1, R):
+        delta_moves.append(
+            start(
+                pltpu.make_async_remote_copy(
+                    src_ref=delta_out.at[k],
+                    dst_ref=delta_in.at[k - 1],
+                    send_sem=r_send.at[2, k],
+                    recv_sem=r_recv.at[2, k],
+                    device_id={"replica": lax.rem(r - k + R, R)},
+                    device_id_type=MESH,
+                )
+            )
+        )
+
+    attend(t, query_ref, 0)
+
+    fresh = base_out[t].astype(jnp.float32) + delta_out[0]
+    for move in base_moves:
+        move.wait_recv()
+    for k in range(1, T):
+        fresh = fresh + base_in[k - 1].astype(jnp.float32)
+    for move in delta_moves:
+        move.wait_recv()
+    for k in range(1, R):
+        fresh = fresh + delta_in[k - 1]
+    fresh = fresh.astype(jnp.bfloat16)
+    fresh_ref[...] = fresh
+    fresh_all[t] = fresh
+    fresh_moves = [
+        start(along_t(5, k, fresh_all.at[t], fresh_all.at[t])) for k in range(1, T)
+    ]
+    for move in fresh_moves:
+        move.wait_recv()
+    for move in acc_moves + lse_moves:
+        move.wait_recv()
+
+    line = lax.broadcasted_iota(jnp.int32, (per_block, tokens), 0)
+    spot = lax.broadcasted_iota(jnp.int32, (per_block, tokens), 1)
+    seen = (line // per_row == spot % row_total) & (spot // row_total <= (line % per_row) // GROUP)
+    for b in range(blocks):
+        column = (t * blocks + b) * HEAD_SIZE
+        holder, offset = column // columns, lax.rem(column, columns)
+        cols = pl.ds(pl.multiple_of(offset, HEAD_SIZE), HEAD_SIZE)
+        new_keys = fresh_all[holder, :, cols]
+        new_values = fresh_all[T // 2 + holder, :, cols]
+        rows = slice(b * per_block, (b + 1) * per_block)
+        scores = scale * lax.dot_general(
+            query_ref[rows, :], new_keys, contract, preferred_element_type=jnp.float32
+        )
+        scores = jnp.where(seen, scores, MASKED)
+        top = jnp.max(scores, axis=1, keepdims=True)
+        levels = []
+        for k in range(T):
+            held = lse_out[0] if k == 0 else lse_in[k - 1]
+            levels.append(
+                jnp.concatenate(
+                    [
+                        held[:, b * row_total + i : b * row_total + i + 1]
+                        for i in range(row_total)
+                    ],
+                    axis=0,
+                )
+            )
+            top = jnp.maximum(top, levels[-1])
+        wide = jnp.where(seen, jnp.exp(scores - top), 0.0)
+        whole = jnp.sum(wide, axis=1, keepdims=True)
+        acc = jnp.dot(wide.astype(jnp.bfloat16), new_values, preferred_element_type=jnp.float32)
+        for k in range(T):
+            factor = jnp.exp(levels[k] - top)
+            held = acc_out[0, rows, :] if k == 0 else acc_in[k - 1, rows, :]
+            whole = whole + factor
+            acc = acc + factor * held.astype(jnp.float32)
+        out_ref[rows, :] = (acc / whole).astype(jnp.bfloat16)
+
+    for copy in started:
+        copy.wait_send()
+
+
+def fused(
+    tensor_size,
+    replica_size,
+    hidden,
+    queries,
+    stored_keys,
+    stored_values,
+    lengths,
+    adapter_of_row,
+    key_value_weight,
+    adapter_down_weight,
+    adapter_up_weight,
+):
+    T, R = tensor_size, replica_size
+    step_total, row_total, feat = hidden.shape
+    adapters, rank_pair, _ = adapter_down_weight.shape
+    columns = adapter_up_weight.shape[2]
+    tokens = step_total * row_total
+    heads_here = queries.shape[2] // HEAD_SIZE
+    blocks = heads_here // GROUP
+    lines = tokens * heads_here
+    per_row = step_total * GROUP
+    arranged = (
+        queries.reshape(step_total, row_total, blocks, GROUP, HEAD_SIZE)
+        .transpose(2, 1, 0, 3, 4)
+        .reshape(lines, HEAD_SIZE)
+    )
+    bf16, f32 = jnp.bfloat16, jnp.float32
+    vmem = pl.BlockSpec(memory_space=pltpu.VMEM)
+    smem = pl.BlockSpec(memory_space=pltpu.SMEM)
+    hbm = pl.BlockSpec(memory_space=pl.ANY)
+    attended, fresh = pl.pallas_call(
+        functools.partial(fused_kernel, T, R, row_total),
+        out_shape=(
+            jax.ShapeDtypeStruct((lines, HEAD_SIZE), bf16),
+            jax.ShapeDtypeStruct((tokens, columns), bf16),
+        ),
+        in_specs=[smem, smem, vmem, vmem, vmem, hbm, hbm, hbm, hbm],
+        out_specs=(vmem, vmem),
+        scratch_shapes=[
+            pltpu.VMEM(stored_keys.shape, bf16),
+            pltpu.VMEM(stored_values.shape, bf16),
+            pltpu.VMEM((adapters * rank_pair, feat), bf16),
+            pltpu.VMEM(key_value_weight.shape, bf16),
+            pltpu.VMEM((T - 1, lines, HEAD_SIZE), bf16),
+            pltpu.VMEM((R - 1, tokens, feat), bf16),
+            pltpu.VMEM((R, row_total, 128), jnp.int32),
+            pltpu.VMEM((T, tokens, columns), bf16),
+            pltpu.VMEM((T - 1, tokens, columns), bf16),
+            pltpu.VMEM((R, tokens, adapters * rank_pair), f32),
+            pltpu.VMEM((T - 1, R, tokens, adapters * rank_pair), f32),
+            pltpu.VMEM((adapters, rank_pair, columns), bf16),
+            pltpu.VMEM((R, tokens, columns), f32),
+            pltpu.VMEM((R - 1, tokens, columns), f32),
+            pltpu.VMEM((T, tokens, columns), bf16),
+            pltpu.VMEM((T, lines, HEAD_SIZE), bf16),
+            pltpu.VMEM((T - 1, lines, HEAD_SIZE), bf16),
+            pltpu.VMEM((T, per_row, 128), f32),
+            pltpu.VMEM((T - 1, per_row, 128), f32),
+            pltpu.SemaphoreType.DMA((3,)),
+            pltpu.SemaphoreType.DMA((CHUNKS,)),
+            pltpu.SemaphoreType.DMA((6, T)),
+            pltpu.SemaphoreType.DMA((6, T)),
+            pltpu.SemaphoreType.DMA((3, R)),
+            pltpu.SemaphoreType.DMA((3, R)),
+        ],
+        compiler_params=pltpu.CompilerParams(
+            collective_id=0, has_side_effects=True, vmem_limit_bytes=48 * 1024 * 1024
+        ),
+        name="fused",
+    )(
+        lengths,
+        adapter_of_row,
+        hidden.reshape(tokens, feat),
+        arranged,
+        adapter_up_weight,
+        stored_keys,
+        stored_values,
+        adapter_down_weight.reshape(adapters * rank_pair, feat),
+        key_value_weight,
+    )
+    attended = (
+        attended.reshape(blocks, row_total, step_total, GROUP, HEAD_SIZE)
+        .transpose(2, 1, 0, 3, 4)
+        .reshape(step_total, row_total, heads_here * HEAD_SIZE)
+    )
+    return (attended, fresh.reshape(step_total, row_total, columns))
+
+
+def fits(tensor_size, hidden, queries, stored_keys, key_value_weight, down, up):
+    heads_here = queries.shape[2] // HEAD_SIZE
+    columns = up.shape[2]
+    pieces = (hidden, stored_keys, stored_keys, key_value_weight, down)
+    return (
+        hidden.shape[0] * hidden.shape[1] == 16
+        and hidden.shape[1] == 8
+        and heads_here % GROUP == 0
+        and columns % HEAD_SIZE == 0
+        and tensor_size % 2 == 0
+        and down.shape[0] * down.shape[1] == 128
+        and up.shape[1] % 16 == 0
+        and hidden.shape[2] % (CHUNKS * 128) == 0
+        and heads_here // GROUP * hidden.shape[1] <= 128
+        and sum(2 * piece.size for piece in pieces) <= 24 * 1024 * 1024
+    )
+
+
+def dispatch(tensor_size, replica_size, *args):
+    hidden, queries, stored_keys = args[:3]
+    key_value_weight, down, up = args[6:]
+    if fits(tensor_size, hidden, queries, stored_keys, key_value_weight, down, up):
+        return fused(tensor_size, replica_size, *args)
+    return per_device(*args)
+
+
 def solution(mesh):
     placed = (
         P(None, ("groups", "replica"), "tensor"),
@@ -173,7 +582,7 @@
         P("replica", None, "tensor"),
     )
     return jax.shard_map(
-        per_device,
+        functools.partial(dispatch, mesh.shape["tensor"], mesh.shape["replica"]),
         mesh=mesh,
         in_specs=placed,
         out_specs=(

time: 216 us -> 54.9 us (0.25)
  waiting for transfers between devices: 106 us -> 0 us
  blocking collectives: 56.7 us -> 0 us
  Pallas kernels: 0 us -> 44.9 us
  matrix products: 13.7 us -> 0 us
  between operations: 14.2 us -> 0.66 us
  other arithmetic: 8.73 us -> 0 us
  local copies, waits for them, and re-layouts: 15.4 us -> 8.96 us
    all_gather x3 -> x0, waiting for transfers between devices: 83.4 us -> none  [the longest x1 72.1 us: joined(): pieces = jax.tree.map(lambda part: lax.all_gather(part, axis), value)]
    all_gather x4 -> x0, blocking collectives: 56.7 us -> none  [the longest x2 26.2 us: joined(): pieces = jax.tree.map(lambda part: lax.all_gather(part, axis), value)]
    pallas_call x0 -> x1, Pallas kernels: none -> 44.9 us  [fused(): pl.pallas_call(functools.partial(fused_kernel, T, R, row_total), out_shap...]
    psum x1 -> x0, waiting for transfers between devices: 22 us -> none  [per_device(): summed = lax.psum((base_part + low_delta).astype(jnp.bfloat16), 'tensor')]
    dot_general x8 -> x0, matrix products: 13.7 us -> none  [the longest x1 8.68 us: per_device(): jnp.dot(hidden.reshape(step_total * row_total, feat_count), key_value_wei...]
    add x8 -> x0, other arithmetic: 6.7 us -> none  [the longest x3 6.6 us: combine_partial(): first_acc * first_factor[..., None] + second_acc * second_factor[..., None]]
    unnamed x19 -> x15, local copies, waits for them, and re-layouts: 2.96 us -> 7.33 us
    slice x5 -> x0, local copies, waits for them, and re-layouts: 3.94 us -> none  [joined(): tail = jax.tree.map(lambda part: part[1:], pieces)]
  transfers between devices with their start and end apart: 4 -> 0, of which waited for: 3 -> 0; matrix products, arithmetic and copies ran while one was open for 15% -> 0% of each run, Pallas kernels for 0% -> 0%
where the time goes in v1:
time: 54.9 us; the launch traced here: 54.5 us
  Pallas kernels  44.9 us (82%)
  local copies, waits for them, and re-layouts  8.96 us (16%)
  between operations  0.66 us (1%)
    pallas_call x1, Pallas kernels, fused(): pl.pallas_call(functools.partial(fused_kernel, T, R, row_total), out_shap...  44.9 us
    unnamed x15, local copies, waits for them, and re-layouts  7.33 us

profile of v1, /device:TPU:0, one launch (start us, length us, event | category | flops | bytes accessed | tf_op | source)
XLA Modules:
  0.0 54.5 jit_solution(17860981033034099935)
XLA Ops:
  0.6 0.9 %copy.11 = bf16[2,8,2,16,128]{4,3,0,1,2:T(8,128)(2,1)S(1)} copy(bf16[2,8,2,16,128]{4,1,3,2,0:T(8,128)(2,1)} %bitcast.16) | data formatting | bytes 262144 | tf_op jit(solution)/shard_map/reshape | solution.py:480
  1.6 0.0 copy-start
  1.6 1.2 %copy-done = bf16[8,64,1024]{2,1,0:T(8,128)(2,1)S(1)} copy-done((bf16[8,64,1024]{2,1,0:T(8,128)(2,1)S(1)}, bf16[8,64,1024]{2,1,0:T(8,128)(2,1)}, u32[]{:S(2)}) %copy-start) | copy-done | bytes 1048600
  2.8 0.0 copy-start.1
  2.8 1.2 %copy-done.1 = bf16[8,64,1024]{2,1,0:T(8,128)(2,1)S(1)} copy-done((bf16[8,64,1024]{2,1,0:T(8,128)(2,1)S(1)}, bf16[8,64,1024]{2,1,0:T(8,128)(2,1)}, u32[]{:S(2)}) %copy-start.1) | copy-done | bytes 1048600
  4.0 0.0 copy-start.2
  4.0 1.2 %copy-done.2 = bf16[4,32,4096]{2,1,0:T(8,128)(2,1)S(1)} copy-done((bf16[4,32,4096]{2,1,0:T(8,128)(2,1)S(1)}, bf16[4,32,4096]{2,1,0:T(8,128)(2,1)}, u32[]{:S(2)}) %copy-start.2) | copy-done | bytes 1048600
  5.2 0.0 copy-start.3
  5.2 0.9 %copy-done.3 = bf16[2,8,4096]{2,1,0:T(8,128)(2,1)S(1)} copy-done((bf16[2,8,4096]{2,1,0:T(8,128)(2,1)S(1)}, bf16[2,8,4096]{2,1,0:T(8,128)(2,1)}, u32[]{:S(2)}) %copy-start.3) | copy-done | bytes 131096
  6.1 0.0 copy-start.4
  6.1 0.8 %copy-done.4 = bf16[4,16,512]{2,1,0:T(8,128)(2,1)S(1)} copy-done((bf16[4,16,512]{2,1,0:T(8,128)(2,1)S(1)}, bf16[4,16,512]{2,1,0:T(8,128)(2,1)}, u32[]{:S(2)}) %copy-start.4) | copy-done | bytes 65560
  7.0 0.0 copy-start.5
  7.0 0.7 %copy-done.5 = s32[8]{0:T(128)S(1)} copy-done((s32[8]{0:T(128)S(1)}, s32[8]{0:T(128)}, u32[]{:S(2)}) %copy-start.5) | copy-done | bytes 56
  7.6 0.0 copy-start.6
  7.6 0.7 %copy-done.6 = s32[8]{0:T(128)S(1)} copy-done((s32[8]{0:T(128)S(1)}, s32[8]{0:T(128)}, u32[]{:S(2)}) %copy-start.6) | copy-done | bytes 56
  8.3 44.9 %fused.1 = (bf16[512,128]{1,0:T(8,128)(2,1)S(1)}, bf16[16,512]{1,0:T(8,128)(2,1)S(1)}) custom-call(s32[8]{0:T(128)S(1)} %copy-done.5, s32[8]{0:T(128)S(1)} %copy-done.6, bf16[16,4096]{1,0:T(8,128)(2,1)S(1)} %bitcast.13, bf16[512,128]{1,0:T(8,128)(2,1)S(1)} %bitcast.12, bf16[4,16,512]{2,1,0:T(8,128)(2,1)S(1)} %copy-done.4, bf16[8,64,1024]{2,1,0:T(8,128)(2,1)S(1)} %copy-done, ...), custom_call_target="tpu_custom_call" | custom-call | tf_op jit(solution)/shard_map/fused/pallas_call | solution.py:488
  53.2 0.7 %copy.12 = bf16[2,8,2,16,128]{4,1,3,2,0:T(8,128)(2,1)} copy(bf16[2,8,2,16,128]{4,3,0,1,2:T(8,128)(2,1)S(1)} %bitcast.14) | data formatting | bytes 262144 | tf_op jit(solution)/shard_map/transpose | solution.py:540
  53.9 0.6 %copy.14 = bf16[2,8,512]{2,1,0:T(8,128)(2,1)} copy(bf16[2,8,512]{2,1,0:T(8,128)(2,1)S(1)} %bitcast.15) | data formatting | bytes 32768
Async XLA Ops:
  1.6 1.2 %copy-start = (bf16[8,64,1024]{2,1,0:T(8,128)(2,1)S(1)}, bf16[8,64,1024]{2,1,0:T(8,128)(2,1)}, u32[]{:S(2)}) copy-start(bf16[8,64,1024]{2,1,0:T(8,128)(2,1)} %key_hbm.1) | copy-start | bytes 3145732
  2.8 1.2 %copy-start.1 = (bf16[8,64,1024]{2,1,0:T(8,128)(2,1)S(1)}, bf16[8,64,1024]{2,1,0:T(8,128)(2,1)}, u32[]{:S(2)}) copy-start(bf16[8,64,1024]{2,1,0:T(8,128)(2,1)} %value_hbm.1) | copy-start | bytes 3145732
  4.0 1.2 %copy-start.2 = (bf16[4,32,4096]{2,1,0:T(8,128)(2,1)S(1)}, bf16[4,32,4096]{2,1,0:T(8,128)(2,1)}, u32[]{:S(2)}) copy-start(bf16[4,32,4096]{2,1,0:T(8,128)(2,1)} %param.16) | copy-start | bytes 3145732
  5.2 0.9 %copy-start.3 = (bf16[2,8,4096]{2,1,0:T(8,128)(2,1)S(1)}, bf16[2,8,4096]{2,1,0:T(8,128)(2,1)}, u32[]{:S(2)}) copy-start(bf16[2,8,4096]{2,1,0:T(8,128)(2,1)} %param.9) | copy-start | bytes 393220
  6.1 0.8 %copy-start.4 = (bf16[4,16,512]{2,1,0:T(8,128)(2,1)S(1)}, bf16[4,16,512]{2,1,0:T(8,128)(2,1)}, u32[]{:S(2)}) copy-start(bf16[4,16,512]{2,1,0:T(8,128)(2,1)} %up_ref.1) | copy-start | bytes 196612
  7.0 0.7 %copy-start.5 = (s32[8]{0:T(128)S(1)}, s32[8]{0:T(128)}, u32[]{:S(2)}) copy-start(s32[8]{0:T(128)} %lengths_ref.1) | copy-start | bytes 100
  7.6 0.7 %copy-start.6 = (s32[8]{0:T(128)S(1)}, s32[8]{0:T(128)}, u32[]{:S(2)}) copy-start(s32[8]{0:T(128)} %ids_ref.1) | copy-start | bytes 100

commit v2 on v1

--- a/solution.py
+++ b/solution.py
@@ -168,21 +168,39 @@
 CHUNKS = 8
 
 
+def rows_at_once(row_total, span):
+    batch = max(1, min(row_total, 256 // span))
+    while row_total % batch:
+        batch -= 1
+    return batch
+
+
+def folded(value, width):
+    shift = width
+    while shift < value.shape[1]:
+        value = value + pltpu.roll(value, shift, axis=1)
+        shift *= 2
+    return value
+
+
 def fused_kernel(
     tensor_size,
     replica_size,
     row_total,
     lengths_ref,
     ids_ref,
-    hidden_ref,
+    hidden_hbm,
     query_ref,
-    up_ref,
+    up_hbm,
     key_hbm,
     value_hbm,
     down_hbm,
     weight_hbm,
     out_ref,
     fresh_ref,
+    hidden_ref,
+    up_ref,
+    bias,
     key_buf,
     value_buf,
     down_buf,
@@ -212,11 +230,9 @@
     T, R = tensor_size, replica_size
     t = lax.axis_index("tensor")
     r = lax.axis_index("replica")
-    tokens, feat = hidden_ref.shape
+    tokens, feat = hidden_hbm.shape
     steps = tokens // row_total
-    columns = up_ref.shape[2]
-    ranks = up_ref.shape[1]
-    adapters = up_ref.shape[0]
+    adapters, ranks, columns = up_hbm.shape
     span = key_buf.shape[1]
     blocks = query_ref.shape[0] // (row_total * steps * GROUP)
     per_row = steps * GROUP
@@ -229,6 +245,10 @@
         pltpu.make_async_copy(key_hbm, key_buf, local_sem.at[1]),
         pltpu.make_async_copy(value_hbm, value_buf, local_sem.at[2]),
     ]
+    small = [
+        pltpu.make_async_copy(hidden_hbm, hidden_ref, local_sem.at[3]),
+        pltpu.make_async_copy(up_hbm, up_ref, local_sem.at[4]),
+    ]
     weights = [
         pltpu.make_async_copy(
             weight_hbm.at[pl.ds(c * depth, depth)],
@@ -237,7 +257,7 @@
         )
         for c in range(CHUNKS)
     ]
-    for copy in weights[:2] + local + weights[2:]:
+    for copy in small + weights[:2] + local + weights[2:]:
         copy.start()
 
     def along_t(kind, k, src, dst, sign=1):
@@ -285,14 +305,27 @@
         started.append(copy)
         return copy
 
+    query_moves = [start(along_t(0, k, query_ref, query_in.at[k - 1])) for k in range(1, T)]
+    small[0].wait()
     hidden_moves = [start(along_r(0, k, hidden_ref, hidden_in.at[k - 1])) for k in range(1, R)]
-    query_moves = [start(along_t(0, k, query_ref, query_in.at[k - 1])) for k in range(1, T)]
     ids_moves = [start(along_r(1, k, ids_in.at[0], ids_in.at[k])) for k in range(1, R)]
 
     up_wide[...] = jnp.zeros_like(up_wide)
     half = (t * columns) // (T * columns // 2)
+    small[1].wait()
     for a in range(adapters):
         up_wide[a, pl.ds(pl.multiple_of(half * ranks, ranks), ranks), :] = up_ref[a]
+
+    batch = rows_at_once(row_total, span)
+    tall, broad = batch * per_row, batch * span
+    line = lax.broadcasted_iota(jnp.int32, (tall, broad), 0) // per_row
+    spot = lax.broadcasted_iota(jnp.int32, (tall, broad), 1)
+    place = t * span + spot % span
+    for n in range(row_total // batch):
+        limit = jnp.zeros((tall, broad), jnp.int32)
+        for i in range(batch):
+            limit = jnp.where(line == i, lengths_ref[n * batch + i], limit)
+        bias[n] = jnp.where((line == spot // span) & (place < limit), 0.0, MASKED)
 
     total = None
     for c in range(CHUNKS):
@@ -312,45 +345,62 @@
 
     local[0].wait()
     contract = (((1,), (1,)), ((), ()))
+    token_lane = lax.broadcasted_iota(jnp.int32, (tokens, 128), 1)
+    pair = 2 * ranks
+    low = jnp.zeros((tokens, 128), jnp.float32)
     for k in range(R):
         if k > 0:
             hidden_moves[k - 1].wait_recv()
+            ids_moves[k - 1].wait_recv()
         tokens_here = hidden_ref[...] if k == 0 else hidden_in[k - 1]
-        low_out[k] = lax.dot_general(
+        features = lax.dot_general(
             tokens_here, down_buf[...], contract, preferred_element_type=jnp.float32
         )
+        mine = ids_in[k] == r * adapters + lane // pair
+        features = jnp.where(jnp.concatenate([mine] * steps, axis=0), features, 0.0)
+        low = jnp.where(token_lane // pair == k, folded(features, pair), low)
+    low_out[...] = low
     low_moves = [start(along_t(2, k, low_out, low_in.at[k - 1])) for k in range(1, T)]
 
     local[1].wait()
     local[2].wait()
-    place = t * span + lax.broadcasted_iota(jnp.int32, (per_row, span), 1)
     lse_lane = lax.broadcasted_iota(jnp.int32, (per_row, 128), 1)
+    count = blocks * row_total
 
     def attend(owner, query, slot):
         lse = jnp.full((per_row, 128), MASKED, jnp.float32)
         for b in range(blocks):
             cols = pl.ds(pl.multiple_of((owner * blocks + b) * HEAD_SIZE, HEAD_SIZE), HEAD_SIZE)
-            for i in range(row_total):
-                first = b * per_block + i * per_row
-                usable = place < lengths_ref[i]
-                scores = scale * lax.dot_general(
-                    query[first : first + per_row, :],
-                    key_buf[i, :, cols],
+            for n in range(row_total // batch):
+                first = b * per_block + n * tall
+                some = pl.ds(n * batch, batch)
+                scores = bias[n] + scale * lax.dot_general(
+                    query[first : first + tall, :],
+                    key_buf[some, :, cols].reshape(broad, HEAD_SIZE),
                     contract,
                     preferred_element_type=jnp.float32,
                 )
-                scores = jnp.where(usable, scores, MASKED)
                 top = jnp.max(scores, axis=1, keepdims=True)
-                wide = jnp.where(usable, jnp.exp(scores - top), 0.0)
-                whole = jnp.maximum(jnp.sum(wide, axis=1, keepdims=True), 1.0)
+                wide = jnp.exp(scores - top)
+                whole = jnp.sum(wide, axis=1, keepdims=True)
                 acc = jnp.dot(
                     wide.astype(jnp.bfloat16),
-                    value_buf[i, :, cols],
+                    value_buf[some, :, cols].reshape(broad, HEAD_SIZE),
                     preferred_element_type=jnp.float32,
                 )
-                acc_out[slot, first : first + per_row, :] = (acc / whole).astype(jnp.bfloat16)
-                lse = jnp.where(lse_lane == b * row_total + i, top + jnp.log(whole), lse)
-        lse_out[slot] = lse
+                acc_out[slot, first : first + tall, :] = (acc * (1.0 / whole)).astype(jnp.bfloat16)
+                level = top + jnp.log(whole)
+                for i in range(batch):
+                    lse = jnp.where(
+                        lse_lane == b * row_total + n * batch + i,
+                        level[i * per_row : (i + 1) * per_row],
+                        lse,
+                    )
+        slab = lse[:8]
+        for v in range(1, per_row // 8):
+            moved = pltpu.roll(lse[8 * v : 8 * v + 8], v * count, axis=1)
+            slab = jnp.where(lane // count == v, moved, slab)
+        lse_out[slot] = slab
 
     acc_moves, lse_moves = [], []
     for k in range(1, T):
@@ -361,14 +411,13 @@
 
     for move in low_moves:
         move.wait_recv()
-    for move in ids_moves:
-        move.wait_recv()
+    packed = low_out[...]
+    for j in range(T - 1):
+        packed = packed + low_in[j]
     wide_up = up_wide[...].reshape(adapters * 2 * ranks, columns)
     for k in range(R):
-        low = low_out[k]
-        for j in range(T - 1):
-            low = low + low_in[j, k]
-        mine = ids_in[k] == r * adapters + lane // (2 * ranks)
+        low = folded(jnp.where(token_lane // pair == k, packed, 0.0), pair)
+        mine = ids_in[k] == r * adapters + lane // pair
         low = jnp.where(jnp.concatenate([mine] * steps, axis=0), low, 0.0)
         high = low.astype(jnp.bfloat16)
         rest = (low - high.astype(jnp.float32)).astype(jnp.bfloat16)
@@ -433,8 +482,9 @@
             levels.append(
                 jnp.concatenate(
                     [
-                        held[:, b * row_total + i : b * row_total + i + 1]
+                        held[:, v * count + b * row_total + i : v * count + b * row_total + i + 1]
                         for i in range(row_total)
+                        for v in range(per_row // 8)
                     ],
                     axis=0,
                 )
@@ -476,6 +526,8 @@
     blocks = heads_here // GROUP
     lines = tokens * heads_here
     per_row = step_total * GROUP
+    span = stored_keys.shape[1]
+    batch = rows_at_once(row_total, span)
     arranged = (
         queries.reshape(step_total, row_total, blocks, GROUP, HEAD_SIZE)
         .transpose(2, 1, 0, 3, 4)
@@ -484,16 +536,19 @@
     bf16, f32 = jnp.bfloat16, jnp.float32
     vmem = pl.BlockSpec(memory_space=pltpu.VMEM)
     smem = pl.BlockSpec(memory_space=pltpu.SMEM)
-    hbm = pl.BlockSpec(memory_space=pl.ANY)
+    hbm = pl.BlockSpec(memory_space=pltpu.HBM)
     attended, fresh = pl.pallas_call(
         functools.partial(fused_kernel, T, R, row_total),
         out_shape=(
             jax.ShapeDtypeStruct((lines, HEAD_SIZE), bf16),
             jax.ShapeDtypeStruct((tokens, columns), bf16),
         ),
-        in_specs=[smem, smem, vmem, vmem, vmem, hbm, hbm, hbm, hbm],
+        in_specs=[smem, smem, hbm, vmem, hbm, hbm, hbm, hbm, hbm],
         out_specs=(vmem, vmem),
         scratch_shapes=[
+            pltpu.VMEM((tokens, feat), bf16),
+            pltpu.VMEM(adapter_up_weight.shape, bf16),
+            pltpu.VMEM((row_total // batch, batch * per_row, batch * span), f32),
             pltpu.VMEM(stored_keys.shape, bf16),
             pltpu.VMEM(stored_values.shape, bf16),
             pltpu.VMEM((adapters * rank_pair, feat), bf16),
@@ -503,17 +558,17 @@
             pltpu.VMEM((R, row_total, 128), jnp.int32),
             pltpu.VMEM((T, tokens, columns), bf16),
             pltpu.VMEM((T - 1, tokens, columns), bf16),
-            pltpu.VMEM((R, tokens, adapters * rank_pair), f32),
-            pltpu.VMEM((T - 1, R, tokens, adapters * rank_pair), f32),
+            pltpu.VMEM((tokens, 128), f32),
+            pltpu.VMEM((T - 1, tokens, 128), f32),
             pltpu.VMEM((adapters, rank_pair, columns), bf16),
             pltpu.VMEM((R, tokens, columns), f32),
             pltpu.VMEM((R - 1, tokens, columns), f32),
             pltpu.VMEM((T, tokens, columns), bf16),
             pltpu.VMEM((T, lines, HEAD_SIZE), bf16),
             pltpu.VMEM((T - 1, lines, HEAD_SIZE), bf16),
-            pltpu.VMEM((T, per_row, 128), f32),
-            pltpu.VMEM((T - 1, per_row, 128), f32),
-            pltpu.SemaphoreType.DMA((3,)),
+            pltpu.VMEM((T, 8, 128), f32),
+            pltpu.VMEM((T - 1, 8, 128), f32),
+            pltpu.SemaphoreType.DMA((5,)),
             pltpu.SemaphoreType.DMA((CHUNKS,)),
             pltpu.SemaphoreType.DMA((6, T)),
             pltpu.SemaphoreType.DMA((6, T)),
@@ -543,7 +598,7 @@
     return (attended, fresh.reshape(step_total, row_total, columns))
 
 
-def fits(tensor_size, hidden, queries, stored_keys, key_value_weight, down, up):
+def fits(tensor_size, replica_size, hidden, queries, stored_keys, key_value_weight, down, up):
     heads_here = queries.shape[2] // HEAD_SIZE
     columns = up.shape[2]
     pieces = (hidden, stored_keys, stored_keys, key_value_weight, down)
@@ -554,9 +609,11 @@
         and columns % HEAD_SIZE == 0
         and tensor_size % 2 == 0
         and down.shape[0] * down.shape[1] == 128
+        and replica_size * down.shape[1] <= 128
         and up.shape[1] % 16 == 0
         and hidden.shape[2] % (CHUNKS * 128) == 0
-        and heads_here // GROUP * hidden.shape[1] <= 128
+        and heads_here // GROUP * hidden.shape[1] * hidden.shape[0] * GROUP <= 1024
+        and 256 % stored_keys.shape[1] == 0
         and sum(2 * piece.size for piece in pieces) <= 24 * 1024 * 1024
     )
 
@@ -564,7 +621,7 @@
 def dispatch(tensor_size, replica_size, *args):
     hidden, queries, stored_keys = args[:3]
     key_value_weight, down, up = args[6:]
-    if fits(tensor_size, hidden, queries, stored_keys, key_value_weight, down, up):
+    if fits(tensor_size, replica_size, hidden, queries, stored_keys, key_value_weight, down, up):
         return fused(tensor_size, replica_size, *args)
     return per_device(*args)
 

time: 54.9 us -> 47.8 us (0.87)
  Pallas kernels: 44.9 us -> 37.8 us
    pallas_call x1, Pallas kernels: 44.9 us -> 37.8 us  [fused(): pl.pallas_call(functools.partial(fused_kernel, T, R, row_total), out_shap...]
where the time goes in v2:
time: 47.8 us; the launch traced here: 47.4 us
  Pallas kernels  37.8 us (79%)
  local copies, waits for them, and re-layouts  8.96 us (19%)
  between operations  0.66 us (1%)
    pallas_call x1, Pallas kernels, fused(): pl.pallas_call(functools.partial(fused_kernel, T, R, row_total), out_shap...  37.8 us
    unnamed x15, local copies, waits for them, and re-layouts  7.33 us

profile of v2, /device:TPU:0, one launch (start us, length us, event | category | flops | bytes accessed | tf_op | source)
XLA Modules:
  0.0 47.4 jit_solution(2967835799908992652)
XLA Ops:
  0.6 0.9 %copy.11 = bf16[2,8,2,16,128]{4,3,0,1,2:T(8,128)(2,1)S(1)} copy(bf16[2,8,2,16,128]{4,1,3,2,0:T(8,128)(2,1)} %bitcast.16) | data formatting | bytes 262144 | tf_op jit(solution)/shard_map/reshape | solution.py:532
  1.6 0.0 copy-start
  1.6 1.2 %copy-done = bf16[8,64,1024]{2,1,0:T(8,128)(2,1)S(1)} copy-done((bf16[8,64,1024]{2,1,0:T(8,128)(2,1)S(1)}, bf16[8,64,1024]{2,1,0:T(8,128)(2,1)}, u32[]{:S(2)}) %copy-start) | copy-done | bytes 1048600
  2.8 0.0 copy-start.1
  2.8 1.2 %copy-done.1 = bf16[8,64,1024]{2,1,0:T(8,128)(2,1)S(1)} copy-done((bf16[8,64,1024]{2,1,0:T(8,128)(2,1)S(1)}, bf16[8,64,1024]{2,1,0:T(8,128)(2,1)}, u32[]{:S(2)}) %copy-start.1) | copy-done | bytes 1048600
  4.0 0.0 copy-start.2
  4.0 1.2 %copy-done.2 = bf16[4,32,4096]{2,1,0:T(8,128)(2,1)S(1)} copy-done((bf16[4,32,4096]{2,1,0:T(8,128)(2,1)S(1)}, bf16[4,32,4096]{2,1,0:T(8,128)(2,1)}, u32[]{:S(2)}) %copy-start.2) | copy-done | bytes 1048600
  5.2 0.0 copy-start.3
  5.2 0.9 %copy-done.3 = bf16[2,8,4096]{2,1,0:T(8,128)(2,1)S(1)} copy-done((bf16[2,8,4096]{2,1,0:T(8,128)(2,1)S(1)}, bf16[2,8,4096]{2,1,0:T(8,128)(2,1)}, u32[]{:S(2)}) %copy-start.3) | copy-done | bytes 131096
  6.1 0.0 copy-start.4
  6.1 0.8 %copy-done.4 = bf16[4,16,512]{2,1,0:T(8,128)(2,1)S(1)} copy-done((bf16[4,16,512]{2,1,0:T(8,128)(2,1)S(1)}, bf16[4,16,512]{2,1,0:T(8,128)(2,1)}, u32[]{:S(2)}) %copy-start.4) | copy-done | bytes 65560
  7.0 0.0 copy-start.5
  7.0 0.7 %copy-done.5 = s32[8]{0:T(128)S(1)} copy-done((s32[8]{0:T(128)S(1)}, s32[8]{0:T(128)}, u32[]{:S(2)}) %copy-start.5) | copy-done | bytes 56
  7.6 0.0 copy-start.6
  7.6 0.7 %copy-done.6 = s32[8]{0:T(128)S(1)} copy-done((s32[8]{0:T(128)S(1)}, s32[8]{0:T(128)}, u32[]{:S(2)}) %copy-start.6) | copy-done | bytes 56
  8.3 37.8 %fused.1 = (bf16[512,128]{1,0:T(8,128)(2,1)S(1)}, bf16[16,512]{1,0:T(8,128)(2,1)S(1)}) custom-call(s32[8]{0:T(128)S(1)} %copy-done.5, s32[8]{0:T(128)S(1)} %copy-done.6, bf16[16,4096]{1,0:T(8,128)(2,1)S(1)} %bitcast.13, bf16[512,128]{1,0:T(8,128)(2,1)S(1)} %bitcast.12, bf16[4,16,512]{2,1,0:T(8,128)(2,1)S(1)} %copy-done.4, bf16[8,64,1024]{2,1,0:T(8,128)(2,1)S(1)} %copy-done, ...), custom_call_target="tpu_custom_call" | custom-call | tf_op jit(solution)/shard_map/fused/pallas_call | solution.py:540
  46.1 0.7 %copy.12 = bf16[2,8,2,16,128]{4,1,3,2,0:T(8,128)(2,1)} copy(bf16[2,8,2,16,128]{4,3,0,1,2:T(8,128)(2,1)S(1)} %bitcast.14) | data formatting | bytes 262144 | tf_op jit(solution)/shard_map/transpose | solution.py:595
  46.8 0.6 %copy.14 = bf16[2,8,512]{2,1,0:T(8,128)(2,1)} copy(bf16[2,8,512]{2,1,0:T(8,128)(2,1)S(1)} %bitcast.15) | data formatting | bytes 32768
Async XLA Ops:
  1.6 1.2 %copy-start = (bf16[8,64,1024]{2,1,0:T(8,128)(2,1)S(1)}, bf16[8,64,1024]{2,1,0:T(8,128)(2,1)}, u32[]{:S(2)}) copy-start(bf16[8,64,1024]{2,1,0:T(8,128)(2,1)} %key_hbm.1) | copy-start | bytes 3145732
  2.8 1.2 %copy-start.1 = (bf16[8,64,1024]{2,1,0:T(8,128)(2,1)S(1)}, bf16[8,64,1024]{2,1,0:T(8,128)(2,1)}, u32[]{:S(2)}) copy-start(bf16[8,64,1024]{2,1,0:T(8,128)(2,1)} %value_hbm.1) | copy-start | bytes 3145732
  4.0 1.2 %copy-start.2 = (bf16[4,32,4096]{2,1,0:T(8,128)(2,1)S(1)}, bf16[4,32,4096]{2,1,0:T(8,128)(2,1)}, u32[]{:S(2)}) copy-start(bf16[4,32,4096]{2,1,0:T(8,128)(2,1)} %param.16) | copy-start | bytes 3145732
  5.2 0.9 %copy-start.3 = (bf16[2,8,4096]{2,1,0:T(8,128)(2,1)S(1)}, bf16[2,8,4096]{2,1,0:T(8,128)(2,1)}, u32[]{:S(2)}) copy-start(bf16[2,8,4096]{2,1,0:T(8,128)(2,1)} %param.9) | copy-start | bytes 393220
  6.1 0.8 %copy-start.4 = (bf16[4,16,512]{2,1,0:T(8,128)(2,1)S(1)}, bf16[4,16,512]{2,1,0:T(8,128)(2,1)}, u32[]{:S(2)}) copy-start(bf16[4,16,512]{2,1,0:T(8,128)(2,1)} %up_hbm.1) | copy-start | bytes 196612
  7.0 0.7 %copy-start.5 = (s32[8]{0:T(128)S(1)}, s32[8]{0:T(128)}, u32[]{:S(2)}) copy-start(s32[8]{0:T(128)} %lengths_ref.1) | copy-start | bytes 100
  7.6 0.7 %copy-start.6 = (s32[8]{0:T(128)S(1)}, s32[8]{0:T(128)}, u32[]{:S(2)}) copy-start(s32[8]{0:T(128)} %ids_ref.1) | copy-start | bytes 100

commit v3 on v2

--- a/solution.py
+++ b/solution.py
@@ -305,7 +305,14 @@
         started.append(copy)
         return copy
 
-    query_moves = [start(along_t(0, k, query_ref, query_in.at[k - 1])) for k in range(1, T)]
+    parts = [pl.ds(b * per_block, per_block) for b in range(blocks)]
+    query_moves = [
+        [
+            start(along_t(6 + b, k, query_ref.at[parts[b]], query_in.at[k - 1, parts[b]]))
+            for k in range(1, T)
+        ]
+        for b in range(blocks)
+    ]
     small[0].wait()
     hidden_moves = [start(along_r(0, k, hidden_ref, hidden_in.at[k - 1])) for k in range(1, R)]
     ids_moves = [start(along_r(1, k, ids_in.at[0], ids_in.at[k])) for k in range(1, R)]
@@ -367,47 +374,58 @@
     lse_lane = lax.broadcasted_iota(jnp.int32, (per_row, 128), 1)
     count = blocks * row_total
 
-    def attend(owner, query, slot):
-        lse = jnp.full((per_row, 128), MASKED, jnp.float32)
-        for b in range(blocks):
-            cols = pl.ds(pl.multiple_of((owner * blocks + b) * HEAD_SIZE, HEAD_SIZE), HEAD_SIZE)
-            for n in range(row_total // batch):
-                first = b * per_block + n * tall
-                some = pl.ds(n * batch, batch)
-                scores = bias[n] + scale * lax.dot_general(
-                    query[first : first + tall, :],
-                    key_buf[some, :, cols].reshape(broad, HEAD_SIZE),
-                    contract,
-                    preferred_element_type=jnp.float32,
+    def attend(owner, query, slot, b, lse):
+        cols = pl.ds(pl.multiple_of((owner * blocks + b) * HEAD_SIZE, HEAD_SIZE), HEAD_SIZE)
+        for n in range(row_total // batch):
+            first = b * per_block + n * tall
+            some = pl.ds(n * batch, batch)
+            scores = bias[n] + scale * lax.dot_general(
+                query[first : first + tall, :],
+                key_buf[some, :, cols].reshape(broad, HEAD_SIZE),
+                contract,
+                preferred_element_type=jnp.float32,
+            )
+            top = jnp.max(scores, axis=1, keepdims=True)
+            wide = jnp.exp(scores - top)
+            whole = jnp.sum(wide, axis=1, keepdims=True)
+            acc = jnp.dot(
+                wide.astype(jnp.bfloat16),
+                value_buf[some, :, cols].reshape(broad, HEAD_SIZE),
+                preferred_element_type=jnp.float32,
+            )
+            acc_out[slot, first : first + tall, :] = (acc * (1.0 / whole)).astype(jnp.bfloat16)
+            level = top + jnp.log(whole)
+            for i in range(batch):
+                lse = jnp.where(
+                    lse_lane == b * row_total + n * batch + i,
+                    level[i * per_row : (i + 1) * per_row],
+                    lse,
                 )
-                top = jnp.max(scores, axis=1, keepdims=True)
-                wide = jnp.exp(scores - top)
-                whole = jnp.sum(wide, axis=1, keepdims=True)
-                acc = jnp.dot(
-                    wide.astype(jnp.bfloat16),
-                    value_buf[some, :, cols].reshape(broad, HEAD_SIZE),
-                    preferred_element_type=jnp.float32,
-                )
-                acc_out[slot, first : first + tall, :] = (acc * (1.0 / whole)).astype(jnp.bfloat16)
-                level = top + jnp.log(whole)
-                for i in range(batch):
-                    lse = jnp.where(
-                        lse_lane == b * row_total + n * batch + i,
-                        level[i * per_row : (i + 1) * per_row],
-                        lse,
-                    )
+        return lse
+
+    def pack(lse, slot):
         slab = lse[:8]
         for v in range(1, per_row // 8):
             moved = pltpu.roll(lse[8 * v : 8 * v + 8], v * count, axis=1)
             slab = jnp.where(lane // count == v, moved, slab)
         lse_out[slot] = slab
 
-    acc_moves, lse_moves = [], []
-    for k in range(1, T):
-        query_moves[k - 1].wait_recv()
-        attend(lax.rem(t - k + T, T), query_in.at[k - 1], k)
-        acc_moves.append(start(along_t(3, k, acc_out.at[k], acc_in.at[k - 1], -1)))
-        lse_moves.append(start(along_t(4, k, lse_out.at[k], lse_in.at[k - 1], -1)))
+    levels_of = [jnp.full((per_row, 128), MASKED, jnp.float32)] * T
+    acc_moves, lse_moves = [[] for _ in range(blocks)], []
+
+    def attend_remote(b):
+        for k in range(1, T):
+            query_moves[b][k - 1].wait_recv()
+            owner = lax.rem(t - k + T, T)
+            levels_of[k] = attend(owner, query_in.at[k - 1], k, b, levels_of[k])
+            source, target = acc_out.at[k, parts[b]], acc_in.at[k - 1, parts[b]]
+            acc_moves[b].append(start(along_t(6 + blocks + b, k, source, target, -1)))
+            if b == blocks - 1:
+                pack(levels_of[k], k)
+                lse_moves.append(start(along_t(4, k, lse_out.at[k], lse_in.at[k - 1], -1)))
+
+    for b in range(blocks - 1):
+        attend_remote(b)
 
     for move in low_moves:
         move.wait_recv()
@@ -439,7 +457,7 @@
             )
         )
 
-    attend(t, query_ref, 0)
+    attend_remote(blocks - 1)
 
     fresh = base_out[t].astype(jnp.float32) + delta_out[0]
     for move in base_moves:
@@ -456,15 +474,19 @@
     fresh_moves = [
         start(along_t(5, k, fresh_all.at[t], fresh_all.at[t])) for k in range(1, T)
     ]
-    for move in fresh_moves:
-        move.wait_recv()
-    for move in acc_moves + lse_moves:
+    for b in range(blocks):
+        levels_of[0] = attend(t, query_ref, 0, b, levels_of[0])
+    pack(levels_of[0], 0)
+
+    for move in fresh_moves + lse_moves:
         move.wait_recv()
 
     line = lax.broadcasted_iota(jnp.int32, (per_block, tokens), 0)
     spot = lax.broadcasted_iota(jnp.int32, (per_block, tokens), 1)
     seen = (line // per_row == spot % row_total) & (spot // row_total <= (line % per_row) // GROUP)
     for b in range(blocks):
+        for move in acc_moves[b]:
+            move.wait_recv()
         column = (t * blocks + b) * HEAD_SIZE
         holder, offset = column // columns, lax.rem(column, columns)
         cols = pl.ds(pl.multiple_of(offset, HEAD_SIZE), HEAD_SIZE)
@@ -570,13 +592,13 @@
             pltpu.VMEM((T - 1, 8, 128), f32),
             pltpu.SemaphoreType.DMA((5,)),
             pltpu.SemaphoreType.DMA((CHUNKS,)),
-            pltpu.SemaphoreType.DMA((6, T)),
-            pltpu.SemaphoreType.DMA((6, T)),
+            pltpu.SemaphoreType.DMA((6 + 2 * blocks, T)),
+            pltpu.SemaphoreType.DMA((6 + 2 * blocks, T)),
             pltpu.SemaphoreType.DMA((3, R)),
             pltpu.SemaphoreType.DMA((3, R)),
         ],
         compiler_params=pltpu.CompilerParams(
-            collective_id=0, has_side_effects=True, vmem_limit_bytes=48 * 1024 * 1024
+            collective_id=0, has_side_effects=True, vmem_limit_bytes=64 * 1024 * 1024
         ),
         name="fused",
     )(

time: 47.8 us -> 42.3 us (0.88)
  local copies, waits for them, and re-layouts: 8.96 us -> 4.51 us
  Pallas kernels: 37.8 us -> 36.9 us
    unnamed x15 -> x1, local copies, waits for them, and re-layouts: 7.33 us -> 1.32 us
    transpose x1, local copies, waits for them, and re-layouts: 0.71 us -> 1.61 us  [fused(): attended = attended.reshape(blocks, row_total, step_total, GROUP, HEAD_SI...]
    pallas_call x1, Pallas kernels: 37.8 us -> 36.9 us  [fused(): pl.pallas_call(functools.partial(fused_kernel, T, R, row_total), out_shap...]
    reshape x1, local copies, waits for them, and re-layouts: 0.92 us -> 1.58 us  [fused(): queries.reshape(step_total, row_total, blocks, GROUP, HEAD_SIZE)]
where the time goes in v3:
time: 42.3 us; the launch traced here: 42.1 us
  Pallas kernels  36.9 us (87%)
  local copies, waits for them, and re-layouts  4.51 us (11%)
  between operations  0.64 us (2%)
    pallas_call x1, Pallas kernels, fused(): pl.pallas_call(functools.partial(fused_kernel, T, R, row_total), out_shap...  36.9 us
    transpose x1, local copies, waits for them, and re-layouts, fused(): attended = attended.reshape(blocks, row_total, step_total, GROUP, HEAD_SI...  1.61 us
    reshape x1, local copies, waits for them, and re-layouts, fused(): queries.reshape(step_total, row_total, blocks, GROUP, HEAD_SIZE)  1.58 us
    unnamed x1, local copies, waits for them, and re-layouts  1.32 us

profile of v3, /device:TPU:0, one launch (start us, length us, event | category | flops | bytes accessed | tf_op | source)
XLA Modules:
  0.0 42.1 jit_solution(3732984881451478405)
XLA Ops:
  0.6 1.6 %copy.11 = bf16[2,8,2,16,128]{4,3,0,1,2:T(8,128)(2,1)} copy(bf16[2,8,2,16,128]{4,1,3,2,0:T(8,128)(2,1)} %bitcast.14) | data formatting | bytes 262144 | tf_op jit(solution)/shard_map/reshape | solution.py:554
  2.2 36.9 %fused.1 = (bf16[512,128]{1,0:T(8,128)(2,1)}, bf16[16,512]{1,0:T(8,128)(2,1)}) custom-call(s32[8]{0:T(128)} %lengths_ref.1, s32[8]{0:T(128)} %ids_ref.1, bf16[16,4096]{1,0:T(8,128)(2,1)} %bitcast.13, bf16[512,128]{1,0:T(8,128)(2,1)} %bitcast.12, bf16[4,16,512]{2,1,0:T(8,128)(2,1)} %up_hbm.1, bf16[8,64,1024]{2,1,0:T(8,128)(2,1)} %key_hbm.1, ...), custom_call_target="tpu_custom_call" | custom-call | tf_op jit(solution)/shard_map/fused/pallas_call | solution.py:562
  39.2 1.6 %copy.12 = bf16[2,8,2,16,128]{4,1,3,2,0:T(8,128)(2,1)} copy(bf16[2,8,2,16,128]{4,3,0,1,2:T(8,128)(2,1)} %bitcast.16) | data formatting | bytes 262144 | tf_op jit(solution)/shard_map/transpose | solution.py:617
  40.8 1.3 %copy.14 = bf16[2,8,512]{2,1,0:T(8,128)(2,1)} copy(bf16[2,8,512]{2,1,0:T(8,128)(2,1)} %bitcast.17) | data formatting | bytes 32768

commit v4 on v3

--- a/solution.py
+++ b/solution.py
@@ -168,13 +168,6 @@
 CHUNKS = 8
 
 
-def rows_at_once(row_total, span):
-    batch = max(1, min(row_total, 256 // span))
-    while row_total % batch:
-        batch -= 1
-    return batch
-
-
 def folded(value, width):
     shift = width
     while shift < value.shape[1]:
@@ -190,7 +183,7 @@
     lengths_ref,
     ids_ref,
     hidden_hbm,
-    query_ref,
+    query_hbm,
     up_hbm,
     key_hbm,
     value_hbm,
@@ -199,6 +192,7 @@
     out_ref,
     fresh_ref,
     hidden_ref,
+    query_ref,
     up_ref,
     bias,
     key_buf,
@@ -234,7 +228,7 @@
     steps = tokens // row_total
     adapters, ranks, columns = up_hbm.shape
     span = key_buf.shape[1]
-    blocks = query_ref.shape[0] // (row_total * steps * GROUP)
+    blocks = query_hbm.shape[1] // (GROUP * HEAD_SIZE)
     per_row = steps * GROUP
     per_block = row_total * per_row
     scale = 1.0 / math.sqrt(HEAD_SIZE)
@@ -248,6 +242,7 @@
     small = [
         pltpu.make_async_copy(hidden_hbm, hidden_ref, local_sem.at[3]),
         pltpu.make_async_copy(up_hbm, up_ref, local_sem.at[4]),
+        pltpu.make_async_copy(query_hbm, query_ref, local_sem.at[5]),
     ]
     weights = [
         pltpu.make_async_copy(
@@ -257,7 +252,7 @@
         )
         for c in range(CHUNKS)
     ]
-    for copy in small + weights[:2] + local + weights[2:]:
+    for copy in small[2:] + small[:2] + weights[:2] + local + weights[2:]:
         copy.start()
 
     def along_t(kind, k, src, dst, sign=1):
@@ -306,9 +301,11 @@
         return copy
 
     parts = [pl.ds(b * per_block, per_block) for b in range(blocks)]
+    bands = [pl.ds(b * GROUP * HEAD_SIZE, GROUP * HEAD_SIZE) for b in range(blocks)]
+    small[2].wait()
     query_moves = [
         [
-            start(along_t(6 + b, k, query_ref.at[parts[b]], query_in.at[k - 1, parts[b]]))
+            start(along_t(6 + b, k, query_ref.at[:, bands[b]], query_in.at[k - 1, :, bands[b]]))
             for k in range(1, T)
         ]
         for b in range(blocks)
@@ -323,16 +320,23 @@
     for a in range(adapters):
         up_wide[a, pl.ds(pl.multiple_of(half * ranks, ranks), ranks), :] = up_ref[a]
 
-    batch = rows_at_once(row_total, span)
-    tall, broad = batch * per_row, batch * span
-    line = lax.broadcasted_iota(jnp.int32, (tall, broad), 0) // per_row
-    spot = lax.broadcasted_iota(jnp.int32, (tall, broad), 1)
-    place = t * span + spot % span
-    for n in range(row_total // batch):
-        limit = jnp.zeros((tall, broad), jnp.int32)
-        for i in range(batch):
-            limit = jnp.where(line == i, lengths_ref[n * batch + i], limit)
-        bias[n] = jnp.where((line == spot // span) & (place < limit), 0.0, MASKED)
+    broad = row_total * span
+    line = lax.broadcasted_iota(jnp.int32, (per_block, broad), 0) % row_total
+    spot = lax.broadcasted_iota(jnp.int32, (per_block, broad), 1)
+    limit = jnp.zeros((1, broad), jnp.int32)
+    owner_row = lax.broadcasted_iota(jnp.int32, (1, broad), 1) // span
+    for i in range(row_total):
+        limit = jnp.where(owner_row == i, lengths_ref[i], limit)
+    bias[...] = jnp.where((line == spot // span) & (t * span + spot % span < limit), 0.0, MASKED)
+
+    def lines_of(query, b):
+        return jnp.concatenate(
+            [
+                query[:, h * HEAD_SIZE : (h + 1) * HEAD_SIZE]
+                for h in range(b * GROUP, (b + 1) * GROUP)
+            ],
+            axis=0,
+        )
 
     total = None
     for c in range(CHUNKS):
@@ -376,31 +380,27 @@
 
     def attend(owner, query, slot, b, lse):
         cols = pl.ds(pl.multiple_of((owner * blocks + b) * HEAD_SIZE, HEAD_SIZE), HEAD_SIZE)
-        for n in range(row_total // batch):
-            first = b * per_block + n * tall
-            some = pl.ds(n * batch, batch)
-            scores = bias[n] + scale * lax.dot_general(
-                query[first : first + tall, :],
-                key_buf[some, :, cols].reshape(broad, HEAD_SIZE),
-                contract,
-                preferred_element_type=jnp.float32,
-            )
-            top = jnp.max(scores, axis=1, keepdims=True)
-            wide = jnp.exp(scores - top)
-            whole = jnp.sum(wide, axis=1, keepdims=True)
-            acc = jnp.dot(
-                wide.astype(jnp.bfloat16),
-                value_buf[some, :, cols].reshape(broad, HEAD_SIZE),
-                preferred_element_type=jnp.float32,
-            )
-            acc_out[slot, first : first + tall, :] = (acc * (1.0 / whole)).astype(jnp.bfloat16)
-            level = top + jnp.log(whole)
-            for i in range(batch):
-                lse = jnp.where(
-                    lse_lane == b * row_total + n * batch + i,
-                    level[i * per_row : (i + 1) * per_row],
-                    lse,
-                )
+        scores = bias[...] + scale * lax.dot_general(
+            lines_of(query, b),
+            key_buf[:, :, cols].reshape(broad, HEAD_SIZE),
+            contract,
+            preferred_element_type=jnp.float32,
+        )
+        top = jnp.max(scores, axis=1, keepdims=True)
+        wide = jnp.exp(scores - top)
+        whole = jnp.sum(wide, axis=1, keepdims=True)
+        acc = jnp.dot(
+            wide.astype(jnp.bfloat16),
+            value_buf[:, :, cols].reshape(broad, HEAD_SIZE),
+            preferred_element_type=jnp.float32,
+        )
+        acc_out[slot, b * per_block : (b + 1) * per_block, :] = (acc * (1.0 / whole)).astype(
+            jnp.bfloat16
+        )
+        level = top + jnp.log(whole)
+        for i in range(row_total):
+            piece = level[i * per_row : (i + 1) * per_row]
+            lse = jnp.where(lse_lane == b * row_total + i, piece, lse)
         return lse
 
     def pack(lse, slot):
@@ -483,7 +483,8 @@
 
     line = lax.broadcasted_iota(jnp.int32, (per_block, tokens), 0)
     spot = lax.broadcasted_iota(jnp.int32, (per_block, tokens), 1)
-    seen = (line // per_row == spot % row_total) & (spot // row_total <= (line % per_row) // GROUP)
+    token = line % tokens
+    seen = (token % row_total == spot % row_total) & (spot // row_total <= token // row_total)
     for b in range(blocks):
         for move in acc_moves[b]:
             move.wait_recv()
@@ -494,7 +495,7 @@
         new_values = fresh_all[T // 2 + holder, :, cols]
         rows = slice(b * per_block, (b + 1) * per_block)
         scores = scale * lax.dot_general(
-            query_ref[rows, :], new_keys, contract, preferred_element_type=jnp.float32
+            lines_of(query_ref, b), new_keys, contract, preferred_element_type=jnp.float32
         )
         scores = jnp.where(seen, scores, MASKED)
         top = jnp.max(scores, axis=1, keepdims=True)
@@ -520,7 +521,12 @@
             held = acc_out[0, rows, :] if k == 0 else acc_in[k - 1, rows, :]
             whole = whole + factor
             acc = acc + factor * held.astype(jnp.float32)
-        out_ref[rows, :] = (acc / whole).astype(jnp.bfloat16)
+        done = (acc / whole).astype(jnp.bfloat16)
+        for g in range(GROUP):
+            head = b * GROUP + g
+            out_ref[:, head * HEAD_SIZE : (head + 1) * HEAD_SIZE] = done[
+                g * tokens : (g + 1) * tokens
+            ]
 
     for copy in started:
         copy.wait_send()
@@ -549,12 +555,6 @@
     lines = tokens * heads_here
     per_row = step_total * GROUP
     span = stored_keys.shape[1]
-    batch = rows_at_once(row_total, span)
-    arranged = (
-        queries.reshape(step_total, row_total, blocks, GROUP, HEAD_SIZE)
-        .transpose(2, 1, 0, 3, 4)
-        .reshape(lines, HEAD_SIZE)
-    )
     bf16, f32 = jnp.bfloat16, jnp.float32
     vmem = pl.BlockSpec(memory_space=pltpu.VMEM)
     smem = pl.BlockSpec(memory_space=pltpu.SMEM)
@@ -562,20 +562,21 @@
     attended, fresh = pl.pallas_call(
         functools.partial(fused_kernel, T, R, row_total),
         out_shape=(
-            jax.ShapeDtypeStruct((lines, HEAD_SIZE), bf16),
+            jax.ShapeDtypeStruct((tokens, queries.shape[2]), bf16),
             jax.ShapeDtypeStruct((tokens, columns), bf16),
         ),
-        in_specs=[smem, smem, hbm, vmem, hbm, hbm, hbm, hbm, hbm],
+        in_specs=[smem, smem, hbm, hbm, hbm, hbm, hbm, hbm, hbm],
         out_specs=(vmem, vmem),
         scratch_shapes=[
             pltpu.VMEM((tokens, feat), bf16),
+            pltpu.VMEM((tokens, queries.shape[2]), bf16),
             pltpu.VMEM(adapter_up_weight.shape, bf16),
-            pltpu.VMEM((row_total // batch, batch * per_row, batch * span), f32),
+            pltpu.VMEM((row_total * per_row, row_total * span), f32),
             pltpu.VMEM(stored_keys.shape, bf16),
             pltpu.VMEM(stored_values.shape, bf16),
             pltpu.VMEM((adapters * rank_pair, feat), bf16),
             pltpu.VMEM(key_value_weight.shape, bf16),
-            pltpu.VMEM((T - 1, lines, HEAD_SIZE), bf16),
+            pltpu.VMEM((T - 1, tokens, queries.shape[2]), bf16),
             pltpu.VMEM((R - 1, tokens, feat), bf16),
             pltpu.VMEM((R, row_total, 128), jnp.int32),
             pltpu.VMEM((T, tokens, columns), bf16),
@@ -590,7 +591,7 @@
             pltpu.VMEM((T - 1, lines, HEAD_SIZE), bf16),
             pltpu.VMEM((T, 8, 128), f32),
             pltpu.VMEM((T - 1, 8, 128), f32),
-            pltpu.SemaphoreType.DMA((5,)),
+            pltpu.SemaphoreType.DMA((6,)),
             pltpu.SemaphoreType.DMA((CHUNKS,)),
             pltpu.SemaphoreType.DMA((6 + 2 * blocks, T)),
             pltpu.SemaphoreType.DMA((6 + 2 * blocks, T)),
@@ -605,18 +606,14 @@
         lengths,
         adapter_of_row,
         hidden.reshape(tokens, feat),
-        arranged,
+        queries.reshape(tokens, queries.shape[2]),
         adapter_up_weight,
         stored_keys,
         stored_values,
         adapter_down_weight.reshape(adapters * rank_pair, feat),
         key_value_weight,
     )
-    attended = (
-        attended.reshape(blocks, row_total, step_total, GROUP, HEAD_SIZE)
-        .transpose(2, 1, 0, 3, 4)
-        .reshape(step_total, row_total, heads_here * HEAD_SIZE)
-    )
+    attended = attended.reshape(queries.shape)
     return (attended, fresh.reshape(step_total, row_total, columns))
 
 

time: 42.3 us -> 40.5 us (0.957)
  local copies, waits for them, and re-layouts: 4.51 us -> 2.89 us
    transpose x1 -> x0, local copies, waits for them, and re-layouts: 1.61 us -> none  [fused(): attended = attended.reshape(blocks, row_total, step_total, GROUP, HEAD_SI...]
    reshape x1 -> x0, local copies, waits for them, and re-layouts: 1.58 us -> none  [fused(): queries.reshape(step_total, row_total, blocks, GROUP, HEAD_SIZE)]
    unnamed x1 -> x2, local copies, waits for them, and re-layouts: 1.32 us -> 2.89 us
where the time goes in v4:
time: 40.5 us; the launch traced here: 40.3 us
  Pallas kernels  36.8 us (91%)
  local copies, waits for them, and re-layouts  2.89 us (7%)
  between operations  0.64 us (2%)
    pallas_call x1, Pallas kernels, fused(): pl.pallas_call(functools.partial(fused_kernel, T, R, row_total), out_shap...  36.8 us
    unnamed x2, local copies, waits for them, and re-layouts  2.89 us

profile of v4, /device:TPU:0, one launch (start us, length us, event | category | flops | bytes accessed | tf_op | source)
XLA Modules:
  0.0 40.3 jit_solution(14169150744746891385)
XLA Ops:
  0.6 36.8 %fused.1 = (bf16[16,4096]{1,0:T(8,128)(2,1)}, bf16[16,512]{1,0:T(8,128)(2,1)}) custom-call(s32[8]{0:T(128)} %lengths_ref.1, s32[8]{0:T(128)} %ids_ref.1, bf16[16,4096]{1,0:T(8,128)(2,1)} %bitcast.6, bf16[16,4096]{1,0:T(8,128)(2,1)} %bitcast.7, bf16[4,16,512]{2,1,0:T(8,128)(2,1)} %up_hbm.1, bf16[8,64,1024]{2,1,0:T(8,128)(2,1)} %key_hbm.1, ...), custom_call_target="tpu_custom_call" | custom-call | tf_op jit(solution)/shard_map/fused/pallas_call | solution.py:562
  37.4 1.6 %copy.13 = bf16[2,8,4096]{2,1,0:T(8,128)(2,1)} copy(bf16[2,8,4096]{2,1,0:T(8,128)(2,1)} %bitcast.8) | data formatting | bytes 262144
  39.0 1.3 %copy.14 = bf16[2,8,512]{2,1,0:T(8,128)(2,1)} copy(bf16[2,8,512]{2,1,0:T(8,128)(2,1)} %bitcast.9) | data formatting | bytes 32768
